TPU v7x, 128 devices: a whole 4x4x4 slice. The times are simulated.
128 devices in a mesh: seq: 16 (over y, x), mp: 8 (over z, core).
Axes of the slice: x: 4, y: 4, z: 4, core: 2. Of those that a mesh axis runs over, the one named last changes fastest.
Arguments:
- tokens: bfloat16 [8192, 8192], P('seq', 'mp'), may hold values from -26 to 26
- query_weight: bfloat16 [8192, 4096], P('mp', 'seq'), may hold values from -0.0625 to 0.0625
- key_value_matrix: bfloat16 [8192, 1024], P('mp'), may hold values from -0.0625 to 0.0625
- output_weight: bfloat16 [4096, 8192], P(None, 'mp'), may hold values from -0.09375 to 0.09375
- document_lengths: int32 [16], replicated, may hold values from 1 to 2048, 8192 in all
- block_order: int32 [64], replicated, may hold values from 0 to 63, each once
Outputs:
- layer_out: bfloat16 [8192, 8192], P('seq', 'mp')
Inputs may be any that keep to these rules, and one draw needn't show every extreme that they name: `document_lengths`: they sum to 8192; the longest document has exactly 2048 tokens. A permutation: row block b of the layout (rows b * 128 to b * 128 + 127) holds the window positions block_order[b] * 128 onward, in order.
All inputs are finite; a program needn't handle non-finite values.
Results may differ from a plain program's by a relative error of at most 0.034.
Values may be sent and summed in bfloat16 or wider, within the bound.
A program may use at most 128 MiB of HBM per device.

v0:
```python
import math

import jax
import jax.numpy as jnp
from jax import lax
from jax.sharding import PartitionSpec as P

QUERY_HEADS = 32
KEY_VALUE_HEADS = 4
HEAD_SIZE = 128
BLK = 128


rope_base = 500000.0
neg_large = -1e30


def round_term(term_f32):
    return lax.optimization_barrier(term_f32.astype(jnp.bfloat16)).astype(jnp.float32)


def rotary_pair_turn(value_matrix, token_positions):
    row_count = value_matrix.shape[0]
    shaped = value_matrix.reshape(row_count, -1, HEAD_SIZE)
    half_dim = HEAD_SIZE // 2
    inverse = jnp.exp(
        -(2.0 * jnp.arange(half_dim, dtype=jnp.float32) / HEAD_SIZE)
        * jnp.log(jnp.float32(rope_base))
    )
    angles = token_positions.astype(jnp.float32)[:, None] * inverse[None, :]
    cosine = jnp.cos(angles)[:, None, :]
    sine_part = jnp.sin(angles)[:, None, :]
    first_half = shaped[..., :half_dim]
    second_half = shaped[..., half_dim:]
    turned = jnp.concatenate(
        [
            first_half * cosine - second_half * sine_part,
            second_half * cosine + first_half * sine_part,
        ],
        axis=-1,
    )
    return turned.reshape(row_count, -1)


def place_rows(row_ids, block_order):
    blocks = block_order.shape[0]
    lookup = jnp.where(
        (row_ids // BLK)[:, None] == jnp.arange(blocks, dtype=jnp.int32)[None, :],
        block_order[None, :],
        0,
    )
    return jnp.sum(lookup, axis=1) * BLK + row_ids % BLK


def owner_of(token_positions, document_lengths):
    doc_ends = jnp.cumsum(document_lengths)
    return jnp.sum((doc_ends[None, :] <= token_positions[:, None]).astype(jnp.int32), axis=1)


def attend(queries, key_values, query_position, query_document, key_position, key_document):
    heads_dev = queries.shape[1] // HEAD_SIZE
    query_count = queries.shape[0]
    key_count = key_values.shape[0]
    flat_rows = query_count * heads_dev
    query_tile = 1024
    key_tile = 1024
    flat_queries = queries.reshape(flat_rows // query_tile, query_tile, HEAD_SIZE)
    flat_position = jnp.repeat(query_position, heads_dev).reshape(
        flat_rows // query_tile, query_tile
    )
    flat_document = jnp.repeat(query_document, heads_dev).reshape(
        flat_rows // query_tile, query_tile
    )
    pair_tiles = key_values.reshape(key_count // key_tile, key_tile, 2 * HEAD_SIZE)
    position_tiles = key_position.reshape(key_count // key_tile, key_tile)
    document_tiles = key_document.reshape(key_count // key_tile, key_tile)
    score_scale = 1.0 / math.sqrt(HEAD_SIZE)
    key_packs = (pair_tiles, position_tiles, document_tiles)

    def one_tile(query_pack):
        query_block, block_position, block_document = query_pack

        def allowed_of(tile_position, tile_document):
            return (block_document[:, None] == tile_document[None, :]) & (
                tile_position[None, :] <= block_position[:, None]
            )

        def scores_of(pair_block):
            return (
                jnp.dot(
                    query_block, pair_block[:, :HEAD_SIZE].T, preferred_element_type=jnp.float32
                )
                * score_scale
            )

        def max_step(running, key_pack):
            pair_block, tile_position, tile_document = key_pack
            allowed = allowed_of(tile_position, tile_document)
            scores = scores_of(pair_block)
            running = jnp.maximum(running, jnp.max(jnp.where(allowed, scores, neg_large), axis=1))
            return (running, None)

        row_max, unused_max = lax.scan(
            max_step, jnp.full((query_tile,), neg_large, jnp.float32), key_packs
        )

        def update(carry, key_pack):
            pair_block, tile_position, tile_document = key_pack
            allowed = allowed_of(tile_position, tile_document)
            denominator, accum = carry
            scores = scores_of(pair_block)
            weights = jnp.where(allowed, jnp.exp(scores - row_max[:, None]), 0.0).astype(
                jnp.bfloat16
            )
            denominator = denominator + jnp.sum(weights.astype(jnp.float32), axis=1)
            accum = accum + jnp.dot(
                weights, pair_block[:, HEAD_SIZE:], preferred_element_type=jnp.float32
            )
            carry = (denominator, accum)
            return (carry, None)

        start_state = (
            jnp.zeros((query_tile,), jnp.float32),
            jnp.zeros((query_tile, HEAD_SIZE), jnp.float32),
        )
        final_state, unused_out = lax.scan(update, start_state, key_packs)
        return (final_state[1] / final_state[0][:, None]).astype(jnp.bfloat16)

    attended = lax.map(one_tile, (flat_queries, flat_position, flat_document))
    attended = attended.reshape(query_count, heads_dev * HEAD_SIZE)
    return attended


def body(tokens, query_weight, key_value_matrix, output_weight, document_lengths, block_order):
    seq_rows, slice_width = tokens.shape
    sequence_count = lax.axis_size("seq")
    model_parallel_count = lax.axis_size("mp")
    seq_index = lax.axis_index("seq")
    mp_index = lax.axis_index("mp")
    window = seq_rows * sequence_count
    portion_rows = seq_rows // model_parallel_count
    source_ids = jnp.arange(sequence_count, dtype=jnp.int32)[:, None]
    within_ids = jnp.arange(portion_rows, dtype=jnp.int32)[None, :]
    query_rows = (source_ids * seq_rows + mp_index * portion_rows + within_ids).reshape(-1)
    query_position = place_rows(query_rows, block_order)
    full_query = lax.all_gather(query_weight, "seq", axis=1, tiled=True)
    query_part = jnp.dot(tokens, full_query, preferred_element_type=jnp.float32)
    pair_part = jnp.dot(tokens, key_value_matrix, preferred_element_type=jnp.float32)
    reduced_sum = lax.psum_scatter(
        round_term(jnp.concatenate([query_part, pair_part], axis=1)).astype(jnp.bfloat16),
        "mp",
        scatter_dimension=0,
        tiled=True,
    ).astype(jnp.float32)
    own_rows = (
        seq_index * seq_rows + mp_index * portion_rows + jnp.arange(portion_rows, dtype=jnp.int32)
    )
    local_token_position = place_rows(own_rows, block_order)
    split_point = QUERY_HEADS * HEAD_SIZE
    own_queries = rotary_pair_turn(reduced_sum[:, :split_point], local_token_position).astype(
        jnp.bfloat16
    )
    local_key_rows = rotary_pair_turn(
        reduced_sum[:, split_point : split_point + KEY_VALUE_HEADS * HEAD_SIZE],
        local_token_position,
    ).reshape(portion_rows, KEY_VALUE_HEADS, HEAD_SIZE)
    local_value_rows = reduced_sum[:, split_point + KEY_VALUE_HEADS * HEAD_SIZE :].reshape(
        portion_rows, KEY_VALUE_HEADS, HEAD_SIZE
    )
    local_pair_rows = jnp.concatenate([local_key_rows, local_value_rows], axis=2).astype(
        jnp.bfloat16
    )
    queries = lax.all_to_all(own_queries, "seq", split_axis=1, concat_axis=0, tiled=True)
    token_slots = jnp.repeat(
        local_pair_rows, sequence_count * model_parallel_count // KEY_VALUE_HEADS, axis=1
    ).reshape(portion_rows, sequence_count * model_parallel_count * 2 * HEAD_SIZE)
    key_values = lax.all_to_all(token_slots, ("seq", "mp"), split_axis=1, concat_axis=0, tiled=True)
    key_row_block = jnp.arange(window, dtype=jnp.int32)
    key_position = place_rows(key_row_block, block_order)
    query_document = owner_of(query_position, document_lengths)
    key_document = owner_of(key_position, document_lengths)
    attended = attend(
        queries, key_values, query_position, query_document, key_position, key_document
    )
    rows_home = lax.all_to_all(attended, "seq", split_axis=0, concat_axis=1, tiled=True)
    output = jnp.dot(
        lax.all_gather(rows_home, "mp", axis=0, tiled=True),
        output_weight,
        preferred_element_type=jnp.float32,
    )
    return output.astype(jnp.bfloat16)


def solution(mesh):
    placed = (P("seq", "mp"), P("mp", "seq"), P("mp", None), P(None, "mp"), P(), P())
    return jax.shard_map(
        body, mesh=mesh, in_specs=placed, out_specs=P("seq", "mp"), check_vma=False
    )
```

profile of v0, /device:TPU:1, one launch (start us, length us, event | category | flops | bytes accessed | tf_op | source)
XLA Modules:
  0.0 385.5 jit_solution(7827414444605229982)
XLA Ops:
  8.1 2.5 convolution_convert_fusion.2
  10.6 79.5 %all-gather.3.cloned.1.call-done = bf16[1024,4096]{1,0:T(8,128)(2,1)} async-done(((bf16[1024,256]{1,0:T(8,128)(2,1)}), bf16[1024,4096]{1,0:T(8,128)(2,1)}) %all-gather.3.cloned.1.call-update) | async-done | bytes 8388624 | tf_op jit(solution)/shard_map/all_gather | solution.py:146
  90.1 8.2 %convolution_convert_fusion = bf16[512,4096]{1,0:T(8,128)(2,1)S(1)} fusion(bf16[512,1024]{1,0:T(8,128)(2,1)} %param.12, bf16[1024,4096]{1,0:T(8,128)(2,1)} %all-gather.3.cloned.1.call-done), kind=kOutput, calls=%fused_computation.22 | convolution fusion | flops 4297064448 | bytes 13631488 | tf_op jit(solution)/shard_map/dot_general | solution.py:147
  98.3 2.8 pad_maximum_fusion
  102.1 37.0 %reduce-scatter.2.cloned.1.call-done = bf16[64,5120]{1,0:T(8,128)(2,1)} async-done(((bf16[512,5120]{1,0:T(8,128)(2,1)}), bf16[64,5120]{1,0:T(8,128)(2,1)}) %reduce-scatter.2.cloned.1.call-update) | async-done | bytes 655376 | tf_op jit(solution)/shard_map/reduce_scatter | solution.py:149
  142.5 6.5 %all-to-all-start = ((bf16[64,16,256]{2,0,1:T(8,128)(2,1)}), bf16[64,16,256]{2,0,1:T(8,128)(2,1)S(1)}, u32[]{:S(2)}, u32[]{:S(2)}) async-start(bf16[64,16,256]{2,0,1:T(8,128)(2,1)} %copy.19), calls=%async_computation.1 | async-start | bytes 1048576 | tf_op jit(solution)/shard_map/all_to_all | solution.py:173
  150.3 7.8 %all-to-all-done = bf16[64,16,256]{2,0,1:T(8,128)(2,1)S(1)} async-done(((bf16[64,16,256]{2,0,1:T(8,128)(2,1)}), bf16[64,16,256]{2,0,1:T(8,128)(2,1)S(1)}, u32[]{:S(2)}, u32[]{:S(2)}) %all-to-all-start) | async-done | bytes 524320 | tf_op jit(solution)/shard_map/all_to_all | solution.py:173
  158.2 2.5 broadcast_in_dim.110
  160.7 9.3 %all-to-all-start.1 = ((bf16[64,128,256]{2,0,1:T(8,128)(2,1)}), bf16[64,128,256]{2,0,1:T(8,128)(2,1)}, u32[]{:S(2)}, u32[]{:S(2)}) async-start(bf16[64,128,256]{2,0,1:T(8,128)(2,1)} %bitcast.71), calls=%async_computation.2 | async-start | bytes 8388608 | tf_op jit(solution)/shard_map/all_to_all | solution.py:177
  173.0 49.7 %all-to-all-done.1 = bf16[64,128,256]{2,0,1:T(8,128)(2,1)} async-done(((bf16[64,128,256]{2,0,1:T(8,128)(2,1)}), bf16[64,128,256]{2,0,1:T(8,128)(2,1)}, u32[]{:S(2)}, u32[]{:S(2)}) %all-to-all-start.1) | async-done | bytes 4194336 | tf_op jit(solution)/shard_map/all_to_all | solution.py:177
  222.7 100.2 %while.36 = (s32[]{:T(128)}, bf16[2,1024,128]{2,1,0:T(8,128)(2,1)}, s32[2,1024]{1,0:T(2,128)S(1)}, s32[2,1024]{1,0:T(2,128)S(1)}, bf16[2,1024,128]{2,1,0:T(8,128...) while((s32[]{:T(128)}, bf16[2,1024,128]{2,1,0:T(8,128)(2,1)}, ...), condition=%wide.region_14.15_spmd, body=%wide.region_7.14_spmd.sunk | while | flops 821561344 | bytes 10084968 | solution.py:129
  222.8 19.3 %while.37 = (s32[]{:T(128)}, f32[1024]{0:T(1024)S(1)}, s32[1024]{0:T(1024)S(1)}, s32[8,1024]{1,0:T(8,128)S(1)}, s32[8,1024]{1,0:T(8,128)S(1)}, /*index=5*/s32[10...) while((s32[]{:T(128)}, f32[1024]{0:T(1024)S(1)}, ...), condition=%wide.region_10.10_spmd.clone, body=%wide.region_8.9_spmd.clone.sunk | while | flops 274727936 | bytes 1622143 | solution.py:103
  242.1 29.8 %while.38 = (s32[]{:T(128)}, f32[1024]{0:T(1024)S(1)}, f32[1024,128]{1,0:T(8,128)S(1)}, s32[1024]{0:T(1024)S(1)}, s32[8,1024]{1,0:T(8,128)S(1)}, /*index=5*/s32[...) while((s32[]{:T(128)}, f32[1024]{0:T(1024)S(1)}, ...), condition=%wide.region_13.13_spmd.clone, body=%wide.region_11.12_spmd.clone.sunk | while | flops 546571264 | bytes 7131280 | solution.py:126
  243.2 1.7 convert_reduce_fusion.4
  247.0 1.7 convert_reduce_fusion.4
  250.7 1.7 convert_reduce_fusion.4
  254.4 1.7 convert_reduce_fusion.4
  258.1 1.7 convert_reduce_fusion.4
  261.8 1.7 convert_reduce_fusion.4
  265.6 1.7 convert_reduce_fusion.4
  269.3 1.7 convert_reduce_fusion.4
  272.9 19.3 %while.37 = (s32[]{:T(128)}, f32[1024]{0:T(1024)S(1)}, s32[1024]{0:T(1024)S(1)}, s32[8,1024]{1,0:T(8,128)S(1)}, s32[8,1024]{1,0:T(8,128)S(1)}, /*index=5*/s32[10...) while((s32[]{:T(128)}, f32[1024]{0:T(1024)S(1)}, ...), condition=%wide.region_10.10_spmd.clone, body=%wide.region_8.9_spmd.clone.sunk | while | flops 274727936 | bytes 1622143 | solution.py:103
  292.2 29.8 %while.38 = (s32[]{:T(128)}, f32[1024]{0:T(1024)S(1)}, f32[1024,128]{1,0:T(8,128)S(1)}, s32[1024]{0:T(1024)S(1)}, s32[8,1024]{1,0:T(8,128)S(1)}, /*index=5*/s32[...) while((s32[]{:T(128)}, f32[1024]{0:T(1024)S(1)}, ...), condition=%wide.region_13.13_spmd.clone, body=%wide.region_11.12_spmd.clone.sunk | while | flops 546571264 | bytes 7131280 | solution.py:126
  293.3 1.7 convert_reduce_fusion.4
  300.8 1.7 convert_reduce_fusion.4
  304.5 1.7 convert_reduce_fusion.4
  312.0 1.7 convert_reduce_fusion.4
  315.7 1.7 convert_reduce_fusion.4
  319.4 1.7 convert_reduce_fusion.4
  324.2 14.4 %all_to_all.48 = bf16[16,64,256]{2,1,0:T(8,128)(2,1)S(1)} all-to-all(bf16[16,64,256]{2,1,0:T(8,128)(2,1)S(1)} %all_to_all.41), channel_id=1, replica_groups=mesh['seq'=16,'mp'=8] {'seq'}, dimensions={0} | all-to-all | bytes 1048576 | tf_op jit(solution)/shard_map/all_to_all | solution.py:185
  339.4 29.4 %all-gather.5.cloned.1.call-done = bf16[512,4096]{1,0:T(8,128)(2,1)} async-done(((bf16[64,4096]{1,0:T(8,128)(2,1)}), bf16[512,4096]{1,0:T(8,128)(2,1)}) %all-gather.5.cloned.1.call-update) | async-done | bytes 4194320 | tf_op jit(solution)/shard_map/all_gather | solution.py:187
  368.8 10.1 %convolution_convert_fusion.1 = bf16[512,1024]{1,0:T(8,128)(2,1)} fusion(bf16[512,4096]{1,0:T(8,128)(2,1)} %all-gather.5.cloned.1.call-done, bf16[4096,1024]{1,0:T(8,128)(2,1)} %param.15), kind=kOutput, calls=%fused_computation.26 | convolution fusion | flops 4295491584 | bytes 13631488 | tf_op jit(solution)/shard_map/dot_general | solution.py:186
  (207 shorter events, 86.7 us)
Async XLA Ops:
  6.5 1.6 copy-start
  6.5 83.5 %all-gather.3.cloned.1.call-start = ((), (), s32[]{:S(2)}) async-start(), calls=%async_computation.4 | async-start | bytes 8912896 | tf_op jit(solution)/shard_map/all_gather | solution.py:146
  7.3 131.9 %reduce-scatter.2.cloned.1.call-start = ((), (), s32[]{:S(2)}) async-start(), calls=%async_computation.5 | async-start | bytes 5898240 | tf_op jit(solution)/shard_map/reduce_scatter | solution.py:149
  101.1 0.7 copy-start.1
  140.6 8.5 %slice-start = ((bf16[64,5120]{1,0:T(8,128)(2,1)}), bf16[64,512]{1,0:T(8,128)(2,1)S(1)}, s32[]{:S(2)}) async-start(bf16[64,5120]{1,0:T(8,128)(2,1)} %reduce-scatter.2.cloned.1.call-done), calls=%async_computation.7 | async-start | bytes 131072 | tf_op jit(solution)/shard_map/slice | solution.py:167
  142.5 15.6 %all-to-all-start = ((bf16[64,16,256]{2,0,1:T(8,128)(2,1)}), bf16[64,16,256]{2,0,1:T(8,128)(2,1)S(1)}, u32[]{:S(2)}, u32[]{:S(2)}) async-start(bf16[64,16,256]{2,0,1:T(8,128)(2,1)} %copy.19), calls=%async_computation.1 | async-start | bytes 1048576 | tf_op jit(solution)/shard_map/all_to_all | solution.py:173
  160.7 10.0 %copy-start.2 = (s32[16]{0:T(128)S(1)}, s32[16]{0:T(128)}, u32[]{:S(2)}) copy-start(s32[16]{0:T(128)} %param.16) | copy-start | bytes 196
  160.7 62.0 %all-to-all-start.1 = ((bf16[64,128,256]{2,0,1:T(8,128)(2,1)}), bf16[64,128,256]{2,0,1:T(8,128)(2,1)}, u32[]{:S(2)}, u32[]{:S(2)}) async-start(bf16[64,128,256]{2,0,1:T(8,128)(2,1)} %bitcast.71), calls=%async_computation.2 | async-start | bytes 8388608 | tf_op jit(solution)/shard_map/all_to_all | solution.py:177
  170.0 198.8 %all-gather.5.cloned.1.call-start = ((), (), s32[]{:S(2)}) async-start(), calls=%async_computation.6 | async-start | bytes 4718592 | tf_op jit(solution)/shard_map/all_gather | solution.py:187
Sparse Core Ops, SparseCore 0:
  9.5 80.5 all-gather.2
  101.2 37.8 reduce-scatter.1
  339.5 29.2 all-gather.4
where the time goes:
time: 388 us; the launch traced here: 385 us
  waiting for transfers between devices  204 us (53%)
  matrix products  82.2 us (21%)
  local copies, waits for them, and re-layouts  45.1 us (12%)
  starting transfers between devices  16 us (4%)
  blocking collectives  14.4 us (4%)
  between operations  13.4 us (3%)
  other arithmetic  8.61 us (2%)
    all_gather x1, waiting for transfers between devices, body(): full_query = lax.all_gather(query_weight, 'seq', axis=1, tiled=True)  79.5 us
    all_to_all x1, waiting for transfers between devices, body(): lax.all_to_all(token_slots, ('seq', 'mp'), split_axis=1, concat_axis=0, t...  49.7 us
    dot_general x32, matrix products, scores_of(): jnp.dot(query_block, pair_block[:, :HEAD_SIZE].T, preferred_element_type=...  47.9 us
    reduce_scatter x1, waiting for transfers between devices, body(): lax.psum_scatter(round_term(jnp.concatenate([query_part, pair_part], axis...  37 us
    squeeze x32, local copies, waits for them, and re-layouts, one_tile(): lax.scan(max_step, jnp.full((query_tile,), neg_large, jnp.float32), key_p...  34.6 us
    all_gather x1, waiting for transfers between devices, body(): lax.all_gather(rows_home, 'mp', axis=0, tiled=True)  29.4 us
    all_to_all x1, blocking collectives, body(): lax.all_to_all(attended, 'seq', split_axis=0, concat_axis=1, tiled=True)  14.4 us
    dot_general x16, matrix products, update(): jnp.dot(weights, pair_block[:, HEAD_SIZE:], preferred_element_type=jnp.fl...  13.5 us
  transfers between devices with their start and end apart: 5, of which 5 were waited for; matrix products, arithmetic and copies ran while one was open for 2% of the time, Pallas kernels for 0%

commit v1 on v0

v1 whole, which is shorter than its diff:
```python
import functools
import math

import jax
import jax.numpy as jnp
import numpy as np
from jax import lax
from jax.experimental import pallas as pl
from jax.experimental.pallas import tpu as pltpu
from jax.sharding import PartitionSpec as P

MESH = pl.DeviceIdType.MESH
HEAD = 128
BLK = 128
ROWS = 512
WIDTH = 1024
WINDOW_BLOCKS = 17
ROPE_BASE = 500000.0
NEG = -1e30
BF16 = jnp.bfloat16
F32 = jnp.float32


def rope_tables():
    half = HEAD // 2
    inverse = np.exp(-(2.0 * np.arange(half) / HEAD) * np.log(ROPE_BASE))
    within = np.arange(BLK)[:, None] * inverse[None, :]
    start = (np.arange(64) * BLK)[:, None] * inverse[None, :]

    def both(values, sign):
        return np.concatenate([sign * values, values], axis=1).astype(np.float32)

    return (
        both(np.cos(within), 1.0),
        both(np.sin(within), -1.0),
        both(np.cos(start), 1.0),
        both(np.sin(start), -1.0),
    )


def place():
    s = lax.axis_index("seq")
    m = lax.axis_index("mp")
    return s // 4, s % 4, m // 2, m % 2


def at(y, x, z, c, dy=0, dx=0, dz=0, dc=0):
    return (((y + dy) % 4) * 4 + (x + dx) % 4, ((z + dz) % 4) * 2 + (c + dc) % 2)


def greet(here, offsets):
    barrier = pltpu.get_barrier_semaphore()
    for off in offsets:
        pl.semaphore_signal(barrier, inc=1, device_id=at(*here, **off), device_id_type=MESH)
    pl.semaphore_wait(barrier, len(offsets))


class Copies:
    def __init__(self, here, send, recv):
        self.here, self.send, self.recv = here, send, recv
        self.count, self.open = 0, []

    def start(self, src, dst, **off):
        k = self.count
        self.count += 1
        copy = pltpu.make_async_remote_copy(
            src_ref=src,
            dst_ref=dst,
            send_sem=self.send.at[k],
            recv_sem=self.recv.at[k],
            device_id=at(*self.here, **off),
            device_id_type=MESH,
        )
        copy.start()
        self.open.append(copy)
        return copy

    def drain(self):
        for copy in self.open:
            copy.wait_send()


def turn(values, block, tables):
    cr, sr, cb, sb = tables
    c0 = cb[pl.ds(block, 1), :]
    s0 = sb[pl.ds(block, 1), :]
    cosine = c0 * cr[...] - s0 * sr[...]
    sine = s0 * cr[...] + c0 * sr[...]
    return values * cosine + pltpu.roll(values, HEAD // 2, 1) * sine


N_K1 = 55
ALL_OFFSETS = [
    dict(dx=1),
    dict(dx=3),
    dict(dx=2),
    dict(dy=1),
    dict(dy=3),
    dict(dz=1),
    dict(dz=3),
    dict(dz=2),
    dict(dc=1),
]


def project_kernel(
    order, cr, sr, cb, sb, tok, wq, wkv, q_out, kv,
    tx, wy, kv_mine, kv_sib_s, kv_sib_r, kv_z_s, kv_z_r,
    q_mine, q_own, q_sib_s, q_sib_r, q_z_s, q_z_r, send, recv,
):
    here = place()
    y, x, z, c = here
    s = 4 * y + x
    tables = (cr, sr, cb, sb)
    greet(here, ALL_OFFSETS)
    go = Copies(here, send, recv)
    top, low = pl.ds(0, ROWS // 2), pl.ds(ROWS // 2, ROWS // 2)
    wtop, wlow = pl.ds(0, WIDTH // 2), pl.ds(WIDTH // 2, WIDTH // 2)

    w_up_t = go.start(wq.at[wtop], wy.at[y, wtop], dy=1)
    w_dn_l = go.start(wq.at[wlow], wy.at[y, wlow], dy=3)
    t_up_t = go.start(tok.at[top], tx.at[0, top], dx=1)
    t_dn_l = go.start(tok.at[low], tx.at[1, low], dx=3)
    w_up_l = go.start(wq.at[wlow], wy.at[y, wlow], dy=1)
    w_dn_t = go.start(wq.at[wtop], wy.at[y, wtop], dy=3)
    t_up_l = go.start(tok.at[low], tx.at[0, low], dx=1)
    t_dn_t = go.start(tok.at[top], tx.at[1, top], dx=3)

    def pair_part(half, out):
        rows = tok[pl.ds(pl.multiple_of(half * 256, 256), 256), :]
        for g in range(4):
            part = jnp.dot(rows, wkv[:, pl.ds(g * 256, 256)], preferred_element_type=F32)
            for i in range(2):
                h = 2 * g + i
                out[h % 4, :, pl.ds((h // 4) * HEAD, HEAD)] = part[:, i * HEAD : (i + 1) * HEAD].astype(out.dtype)

    pair_part(1 - c, kv_sib_s)
    sib = go.start(kv_sib_s, kv_sib_r, dc=1)
    pair_part(c, kv_mine)
    wy[y] = wq[...]
    sib.wait_recv()
    kv_z = []
    for r in (2, 1, 3):
        d = (z + r) % 4
        kv_z_s[r - 1] = (kv_mine[d] + kv_sib_r[d].astype(F32)).astype(BF16)
        kv_z.append(go.start(kv_z_s.at[r - 1], kv_z_r.at[r - 1], dz=r))
    own_pair = kv_mine[z] + kv_sib_r[z].astype(F32)
    for copy in kv_z:
        copy.wait_recv()
    for r in range(3):
        own_pair = own_pair + kv_z_r[r].astype(F32)
    kv[c, s, :, pl.ds(HEAD, HEAD)] = own_pair[:, HEAD:].astype(BF16)
    for i in range(2):
        block = order[4 * s + 2 * c + i]
        part = own_pair[i * BLK : (i + 1) * BLK, :HEAD]
        kv[c, s, pl.ds(i * BLK, BLK), pl.ds(0, HEAD)] = turn(part, block, tables).astype(BF16)
    kv_x = [go.start(kv.at[c, s], kv.at[c, s], dx=r) for r in (2, 1, 3)]

    w_up_t.wait_recv()
    w_rel_up = go.start(wy.at[(y + 3) % 4, wtop], wy.at[(y + 3) % 4, wtop], dy=1)
    w_dn_l.wait_recv()
    w_rel_dn = go.start(wy.at[(y + 1) % 4, wlow], wy.at[(y + 1) % 4, wlow], dy=3)
    for copy in (w_up_l, w_dn_t, w_rel_up, w_rel_dn):
        copy.wait_recv()

    def project(rows, t):
        def one(g, carry):
            part = jnp.dot(rows[...], wy[g], preferred_element_type=F32)
            first, second = part[:, :HEAD], part[:, HEAD:]
            q_mine[g] = jnp.where(c == 0, first, second)
            q_sib_s[t, g] = jnp.where(c == 0, second, first).astype(BF16)
            return carry

        lax.fori_loop(0, 4, one, 0)
        return go.start(q_sib_s.at[t], q_sib_r.at[t], dc=1)

    def spread(t, copy):
        copy.wait_recv()
        sent = []
        for r in (2, 1, 3):
            d = (z + r) % 4
            q_z_s[t, r - 1] = (q_mine[d] + q_sib_r[t, d].astype(F32)).astype(BF16)
            sent.append(go.start(q_z_s.at[t, r - 1], q_z_r.at[t, r - 1], dz=r))
        q_own[t] = q_mine[z] + q_sib_r[t, z].astype(F32)
        return sent

    scale = math.log2(math.e) / math.sqrt(HEAD)

    def finish(t, shift, sent):
        for copy in sent:
            copy.wait_recv()
        first = 4 * (4 * y + (x + shift) % 4)
        for i in range(4):
            rows = pl.ds(i * BLK, BLK)
            total = q_own[t, rows, :]
            for r in range(3):
                total = total + q_z_r[t, r, rows, :].astype(F32)
            q_out[t, rows, :] = (turn(total, order[first + i], tables) * scale).astype(BF16)

    own_sent = spread(0, project(tok, 0))

    for copy in kv_x:
        copy.wait_recv()
    row = kv.at[c, pl.ds(4 * y, 4)]
    kv_up = go.start(row, row, dy=1)
    kv_dn = go.start(row, row, dy=3)
    kv_sib = [go.start(row, row, dc=1)]

    t_up_t.wait_recv()
    t_rel_up = go.start(tx.at[0, top], tx.at[2, top], dx=1)
    t_dn_l.wait_recv()
    t_rel_dn = go.start(tx.at[1, low], tx.at[2, low], dx=3)
    finish(0, 0, own_sent)
    t_up_l.wait_recv()
    left_sent = spread(1, project(tx.at[0], 1))
    t_dn_t.wait_recv()
    right_sent = spread(2, project(tx.at[1], 2))

    kv_up.wait_recv()
    part = kv.at[c, pl.ds(4 * ((y + 3) % 4), 2)]
    kv_rel_up = go.start(part, part, dy=1)
    kv_dn.wait_recv()
    part = kv.at[c, pl.ds(4 * ((y + 1) % 4) + 2, 2)]
    kv_rel_dn = go.start(part, part, dy=3)
    for r in (1, 3):
        row = kv.at[c, pl.ds(4 * ((y + r) % 4), 4)]
        kv_sib.append(go.start(row, row, dc=1))
    finish(1, 3, left_sent)
    finish(2, 1, right_sent)
    t_rel_up.wait_recv()
    t_rel_dn.wait_recv()
    far_sent = spread(3, project(tx.at[2], 3))
    kv_rel_up.wait_recv()
    kv_rel_dn.wait_recv()
    row = kv.at[c, pl.ds(4 * ((y + 2) % 4), 4)]
    kv_sib.append(go.start(row, row, dc=1))
    finish(3, 2, far_sent)
    for copy in kv_sib:
        copy.wait_recv()
    go.drain()


def project(order, tok, wq, wkv):
    vm = pl.BlockSpec(memory_space=pltpu.VMEM)
    sm = pl.BlockSpec(memory_space=pltpu.SMEM)
    n = 55
    return pl.pallas_call(
        project_kernel,
        out_shape=(
            jax.ShapeDtypeStruct((4, ROWS, HEAD), BF16),
            jax.ShapeDtypeStruct((2, 16, 256, 256), BF16),
        ),
        in_specs=[sm] + [vm] * 7,
        out_specs=(vm, vm),
        scratch_shapes=[
            pltpu.VMEM((3, ROWS, WIDTH), BF16),
            pltpu.VMEM((4, WIDTH, 256), BF16),
            pltpu.VMEM((4, 256, 256), F32),
            pltpu.VMEM((4, 256, 256), BF16),
            pltpu.VMEM((4, 256, 256), BF16),
            pltpu.VMEM((3, 256, 256), BF16),
            pltpu.VMEM((3, 256, 256), BF16),
            pltpu.VMEM((4, ROWS, HEAD), F32),
            pltpu.VMEM((4, ROWS, HEAD), F32),
            pltpu.VMEM((4, 4, ROWS, HEAD), BF16),
            pltpu.VMEM((4, 4, ROWS, HEAD), BF16),
            pltpu.VMEM((4, 3, ROWS, HEAD), BF16),
            pltpu.VMEM((4, 3, ROWS, HEAD), BF16),
            pltpu.SemaphoreType.DMA((n,)),
            pltpu.SemaphoreType.DMA((n,)),
        ],
        compiler_params=pltpu.CompilerParams(
            collective_id=0, has_side_effects=True, vmem_limit_bytes=48 << 20
        ),
    )(order, *[jnp.asarray(t) for t in rope_tables()], tok, wq, wkv)


def attend_kernel(order, where, lengths, q, kv, out, score):
    y, x, z, c = place()

    def one(n, carry):
        t, i = n // 4, n % 4
        shift = jnp.where(t == 0, 0, jnp.where(t == 1, 3, jnp.where(t == 2, 1, 2)))
        block = order[4 * (4 * y + (x + shift) % 4) + i]
        rows = pl.ds(pl.multiple_of(i * BLK, BLK), BLK)
        query = q[t, rows, :]
        pos = lax.broadcasted_iota(jnp.int32, (BLK, BLK), 0) + block * BLK
        lane = lax.broadcasted_iota(jnp.int32, (BLK, BLK), 1)
        begin = jnp.zeros((BLK, BLK), jnp.int32)
        end = jnp.int32(0)
        for d in range(16):
            end = end + lengths[d]
            begin = jnp.where(pos >= end, end, begin)
        base = (block - (WINDOW_BLOCKS - 1)) * BLK
        ahead = lane + (base - begin)
        top = jnp.full((BLK, BLK), NEG, F32)
        offsets = []
        for j in range(WINDOW_BLOCKS):
            held = where[jnp.maximum(block - (WINDOW_BLOCKS - 1) + j, 0)]
            off = (held % 4) // 2 * 4096 + held // 4 * 256 + held % 2 * 128
            off = pl.multiple_of(off, 128)
            offsets.append(off)
            keys = kv[pl.ds(off, BLK), pl.ds(0, HEAD)]
            s = lax.dot_general(query, keys, (((1,), (1,)), ((), ())), preferred_element_type=F32)
            allowed = ahead >= -j * BLK
            if j == WINDOW_BLOCKS - 1:
                allowed = allowed & (lane <= pos - block * BLK)
            s = jnp.where(allowed, s, NEG)
            score[j] = s
            top = jnp.maximum(top, s)
        largest = jnp.max(top, axis=1, keepdims=True)
        total = jnp.zeros((BLK, BLK), F32)
        acc = jnp.zeros((BLK, HEAD), F32)
        for j in range(WINDOW_BLOCKS):
            w = jnp.exp2(score[j] - largest)
            total = total + w
            values = kv[pl.ds(offsets[j], BLK), pl.ds(HEAD, HEAD)]
            acc = acc + jnp.dot(w.astype(BF16), values, preferred_element_type=F32)
        out[t, rows, :] = (acc / jnp.sum(total, axis=1, keepdims=True)).astype(BF16)
        return carry

    lax.fori_loop(0, 16, one, 0)


def attend(order, where, lengths, q, kv):
    vm = pl.BlockSpec(memory_space=pltpu.VMEM)
    sm = pl.BlockSpec(memory_space=pltpu.SMEM)
    return pl.pallas_call(
        attend_kernel,
        out_shape=jax.ShapeDtypeStruct((4, ROWS, HEAD), BF16),
        in_specs=[sm, sm, sm, vm, vm],
        out_specs=vm,
        scratch_shapes=[pltpu.VMEM((WINDOW_BLOCKS, BLK, BLK), F32)],
        compiler_params=pltpu.CompilerParams(vmem_limit_bytes=32 << 20),
    )(order, where, lengths, q, kv.reshape(8192, 256))


OUT_OFFSETS = [
    dict(dx=1),
    dict(dx=3),
    dict(dx=2),
    dict(dz=1),
    dict(dz=3),
    dict(dz=2),
    dict(dc=1),
]


def output_kernel(a, wo_hbm, out, att, wo, acc, local, send, recv):
    here = place()
    y, x, z, c = here
    load = pltpu.make_async_copy(wo_hbm, wo, local)
    load.start()
    greet(here, OUT_OFFSETS)
    go = Copies(here, send, recv)
    home = [
        go.start(a.at[1], att.at[z, c, x], dx=3),
        go.start(a.at[2], att.at[z, c, x], dx=1),
        go.start(a.at[3], att.at[z, c, x], dx=2),
    ]
    att[z, c, x] = a[0]
    lifts = []
    for k, shift in enumerate((0, 1, 3, 2)):
        if k:
            home[k - 1].wait_recv()
        piece = att.at[z, c, (x + shift) % 4]
        lifts.append([go.start(piece, piece, dz=r) for r in (2, 1, 3)])
    sib = [go.start(att.at[z, c], att.at[z, c], dc=1)]
    load.wait()

    def multiply(d, first):
        heads = [att[d, i % 2, i // 2] for i in range(8)]
        left = jnp.concatenate(heads, axis=1)
        depth = pl.ds(pl.multiple_of(d * WIDTH, WIDTH), WIDTH)

        def tile(n, carry):
            cols = pl.ds(pl.multiple_of(n * 256, 256), 256)
            part = jnp.dot(left, wo[depth, cols], preferred_element_type=F32)
            acc[:, cols] = part if first else acc[:, cols] + part
            return carry

        lax.fori_loop(0, 4, tile, 0)

    sib[0].wait_recv()
    multiply(z, True)
    for i, r in ((1, 1), (2, 3), (0, 2)):
        d = (z + 4 - r) % 4
        for lift in lifts:
            lift[i].wait_recv()
        copy = go.start(att.at[d, c], att.at[d, c], dc=1)
        copy.wait_recv()
        multiply(d, False)
    out[...] = acc[...].astype(BF16)
    go.drain()


def project_out(a, wo):
    vm = pl.BlockSpec(memory_space=pltpu.VMEM)
    n = 19
    return pl.pallas_call(
        output_kernel,
        out_shape=jax.ShapeDtypeStruct((ROWS, WIDTH), BF16),
        in_specs=[vm, pl.BlockSpec(memory_space=pl.ANY)],
        out_specs=vm,
        scratch_shapes=[
            pltpu.VMEM((4, 2, 4, ROWS, HEAD), BF16),
            pltpu.VMEM((4 * WIDTH, WIDTH), BF16),
            pltpu.VMEM((ROWS, WIDTH), F32),
            pltpu.SemaphoreType.DMA,
            pltpu.SemaphoreType.DMA((n,)),
            pltpu.SemaphoreType.DMA((n,)),
        ],
        compiler_params=pltpu.CompilerParams(
            collective_id=1, has_side_effects=True, vmem_limit_bytes=32 << 20
        ),
    )(a, wo)


def body(tokens, query_weight, key_value_matrix, output_weight, document_lengths, block_order):
    blocks = jnp.arange(64, dtype=jnp.int32)
    where = jnp.sum(jnp.where(block_order[None, :] == blocks[:, None], blocks[None, :], 0), axis=1)
    q, kv = project(block_order, tokens, query_weight, key_value_matrix)
    a = attend(block_order, where, document_lengths, q, kv)
    return project_out(a, output_weight)


def solution(mesh):
    placed = (P("seq", "mp"), P("mp", "seq"), P("mp", None), P(None, "mp"), P(), P())
    return jax.shard_map(
        body, mesh=mesh, in_specs=placed, out_specs=P("seq", "mp"), check_vma=False
    )
```

time: 388 us -> 143 us (0.37)
  waiting for transfers between devices: 204 us -> 0 us
  Pallas kernels: 0 us -> 131 us
  matrix products: 82.2 us -> 0 us
  local copies, waits for them, and re-layouts: 45.1 us -> 11.5 us
  starting transfers between devices: 16 us -> 0 us
  blocking collectives: 14.4 us -> 0 us
  between operations: 13.4 us -> 0.06 us
  other arithmetic: 8.61 us -> 0.76 us
    pallas_call x0 -> x3, Pallas kernels: none -> 131 us  [the longest x1 69.7 us: project(): pl.pallas_call(project_kernel, out_shape=(jax.ShapeDtypeStruct((4, ROWS,...]
    all_gather x2 -> x0, waiting for transfers between devices: 109 us -> none  [the longest x1 79.5 us: body(): full_query = lax.all_gather(query_weight, 'seq', axis=1, tiled=True)]
    dot_general x51 -> x0, matrix products: 82.2 us -> none  [the longest x32 47.9 us: scores_of(): jnp.dot(query_block, pair_block[:, :HEAD_SIZE].T, preferred_element_type=...]
    all_to_all x2 -> x0, waiting for transfers between devices: 57.5 us -> none  [the longest x1 49.7 us: body(): lax.all_to_all(token_slots, ('seq', 'mp'), split_axis=1, concat_axis=0, t...]
    reduce_scatter x1 -> x0, waiting for transfers between devices: 37 us -> none  [body(): lax.psum_scatter(round_term(jnp.concatenate([query_part, pair_part], axis...]
    squeeze x34 -> x0, local copies, waits for them, and re-layouts: 34.7 us -> none  [the longest x32 34.6 us: one_tile(): lax.scan(max_step, jnp.full((query_tile,), neg_large, jnp.float32), key_p...]
    all_to_all x2 -> x0, starting transfers between devices: 15.8 us -> none  [the longest x1 9.29 us: body(): lax.all_to_all(token_slots, ('seq', 'mp'), split_axis=1, concat_axis=0, t...]
    all_to_all x1 -> x0, blocking collectives: 14.4 us -> none  [body(): lax.all_to_all(attended, 'seq', split_axis=0, concat_axis=1, tiled=True)]
  transfers between devices with their start and end apart: 5 -> 0, of which waited for: 5 -> 0; matrix products, arithmetic and copies ran while one was open for 2% -> 0% of each run, Pallas kernels for 0% -> 0%
where the time goes in v1:
time: 143 us
  Pallas kernels  131 us (92%)
  local copies, waits for them, and re-layouts  11.5 us (8%)
    pallas_call x1, Pallas kernels, project(): pl.pallas_call(project_kernel, out_shape=(jax.ShapeDtypeStruct((4, ROWS,...  69.7 us
    pallas_call x1, Pallas kernels, project_out(): pl.pallas_call(output_kernel, out_shape=jax.ShapeDtypeStruct((ROWS, WIDTH...  39.6 us
    pallas_call x1, Pallas kernels, attend(): pl.pallas_call(attend_kernel, out_shape=jax.ShapeDtypeStruct((4, ROWS, HE...  21.2 us
    unnamed x23, local copies, waits for them, and re-layouts  11.5 us

profile of v1, /device:TPU:1, one launch (start us, length us, event | category | flops | bytes accessed | tf_op | source)
XLA Modules:
  0.0 142.9 jit_solution(3493256606894222821)
XLA Ops:
  0.0 0.8 select_reduce_fusion.where
  0.8 0.0 copy-start.2
  0.8 1.6 %copy-done.2 = bf16[1024,1024]{1,0:T(8,128)(2,1)S(1)} copy-done((bf16[1024,1024]{1,0:T(8,128)(2,1)S(1)}, bf16[1024,1024]{1,0:T(8,128)(2,1)}, u32[]{:S(2)}) %copy-start.2) | copy-done | bytes 2097176
  2.4 0.0 copy-start.3
  2.4 1.2 copy-done.3
  3.6 0.0 copy-start.4
  3.6 1.0 copy-done.4
  4.6 0.0 copy-start.5
  4.6 0.8 copy-done.5
  5.5 0.0 copy-start.6
  5.5 0.8 copy-done.6
  6.3 0.0 copy-start.7
  6.3 0.8 copy-done.7
  7.1 0.0 copy-start.8
  7.1 0.8 copy-done.8
  7.8 0.0 copy-start.9
  7.8 0.7 copy-done.9
  8.5 0.0 copy-start
  8.5 69.7 %shard_map.100 = (bf16[4,512,128]{2,1,0:T(8,128)(2,1)S(1)}, bf16[2,16,256,256]{3,2,1,0:T(8,128)(2,1)}) custom-call(s32[64]{0:T(128)S(1)} %copy-done.9, f32[128,128]{1,0:T(8,128)S(1)} %copy-done.6, f32[128,128]{1,0:T(8,128)S(1)} %copy-done.5, f32[64,128]{1,0:T(8,128)S(1)} %copy-done.8, f32[64,128]{1,0:T(8,128)S(1)} %copy-done.7, ...), custom_call_target="tpu_custom_call" | custom-call | tf_op jit(solution)/shard_map/pallas_call | solution.py:247
  78.2 0.0 copy-start.1
  78.3 2.2 %copy-done.1 = bf16[2,16,256,256]{3,2,1,0:T(8,128)(2,1)S(1)} copy-done((bf16[2,16,256,256]{3,2,1,0:T(8,128)(2,1)S(1)}, bf16[2,16,256,256]{3,2,1,0:T(8,128)(2,1)}, u32[]{:S(2)}) %copy-start.1) | copy-done | bytes 4194328
  80.4 0.0 copy-start.10
  80.4 0.7 copy-done.10
  81.1 21.2 %shard_map.101.a = bf16[4,512,128]{2,1,0:T(8,128)(2,1)S(1)} custom-call(s32[64]{0:T(128)S(1)} %copy-done.9, s32[64]{0:T(128)S(1)} %select_reduce_fusion.where, s32[16]{0:T(128)S(1)} %copy-done.10, bf16[4,512,128]{2,1,0:T(8,128)(2,1)S(1)} %get-tuple-element.7.q, bf16[8192,256]{1,0:T(8,128)(2,1)S(1)} %bitcast.1), custom_call_target="tpu_custom_call" | custom-call | tf_op jit(solution)/shard_map/pallas_call | solution.py:328
  102.3 0.0 copy-done
  102.3 39.6 %shard_map.102 = bf16[512,1024]{1,0:T(8,128)(2,1)S(1)} custom-call(bf16[4,512,128]{2,1,0:T(8,128)(2,1)S(1)} %shard_map.101.a, bf16[4096,1024]{1,0:T(8,128)(2,1)S(1)} %copy-done), custom_call_target="tpu_custom_call" | custom-call | tf_op jit(solution)/shard_map/pallas_call | solution.py:400
  141.9 1.0 copy.12
Async XLA Ops:
  0.8 1.6 %copy-start.2 = (bf16[1024,1024]{1,0:T(8,128)(2,1)S(1)}, bf16[1024,1024]{1,0:T(8,128)(2,1)}, u32[]{:S(2)}) copy-start(bf16[1024,1024]{1,0:T(8,128)(2,1)} %wkv.1) | copy-start | bytes 6291460
  2.4 1.2 copy-start.3
  3.6 1.0 copy-start.4
  4.6 0.8 copy-start.5
  5.5 0.8 copy-start.6
  6.3 0.8 copy-start.7
  7.1 0.8 copy-start.8
  7.8 0.7 copy-start.9
  8.5 93.8 %copy-start = (bf16[4096,1024]{1,0:T(8,128)(2,1)S(1)}, bf16[4096,1024]{1,0:T(8,128)(2,1)}, u32[]{:S(2)}) copy-start(bf16[4096,1024]{1,0:T(8,128)(2,1)} %wo_hbm.1) | copy-start | bytes 25165828
  78.2 2.2 %copy-start.1 = (bf16[2,16,256,256]{3,2,1,0:T(8,128)(2,1)S(1)}, bf16[2,16,256,256]{3,2,1,0:T(8,128)(2,1)}, u32[]{:S(2)}) copy-start(bf16[2,16,256,256]{3,2,1,0:T(8,128)(2,1)} %get-tuple-element.8) | copy-start | bytes 12582916
  80.4 0.7 copy-start.10

commit v2 on v1

v2 whole, which is shorter than its diff:
```python
import functools
import math

import jax
import jax.numpy as jnp
import numpy as np
from jax import lax
from jax.experimental import pallas as pl
from jax.experimental.pallas import tpu as pltpu
from jax.sharding import PartitionSpec as P

MESH = pl.DeviceIdType.MESH
HEAD = 128
BLK = 128
ROWS = 512
WIDTH = 1024
WINDOW_BLOCKS = 17
ROPE_BASE = 500000.0
NEG = -1e30
BF16 = jnp.bfloat16
F32 = jnp.float32


UNITS = ((0, 0), (0, 1), (1, 0), (2, 1), (1, 1), (2, 0), (3, 0), (3, 1))
SHIFT = (0, 3, 1, 2)
HALF = ROWS // 2


def rope_tables():
    half = HEAD // 2
    inverse = np.exp(-(2.0 * np.arange(half) / HEAD) * np.log(ROPE_BASE))
    within = np.arange(BLK)[:, None] * inverse[None, :]
    start = (np.arange(64) * BLK)[:, None] * inverse[None, :]

    def both(values, sign):
        return np.concatenate([sign * values, values], axis=1).astype(np.float32)

    return np.concatenate(
        [
            both(np.cos(within), 1.0),
            both(np.sin(within), -1.0),
            both(np.cos(start), 1.0),
            both(np.sin(start), -1.0),
        ]
    )


def place():
    s = lax.axis_index("seq")
    m = lax.axis_index("mp")
    return s // 4, s % 4, m // 2, m % 2


def at(y, x, z, c, dy=0, dx=0, dz=0, dc=0):
    return (((y + dy) % 4) * 4 + (x + dx) % 4, ((z + dz) % 4) * 2 + (c + dc) % 2)


def greet(here, offsets):
    barrier = pltpu.get_barrier_semaphore()
    for off in offsets:
        pl.semaphore_signal(barrier, inc=1, device_id=at(*here, **off), device_id_type=MESH)
    pl.semaphore_wait(barrier, len(offsets))


class Copies:
    def __init__(self, here, send, recv):
        self.here, self.send, self.recv = here, send, recv
        self.count, self.open = 0, []

    def start(self, src, dst, **off):
        k = self.count
        self.count += 1
        copy = pltpu.make_async_remote_copy(
            src_ref=src,
            dst_ref=dst,
            send_sem=self.send.at[k],
            recv_sem=self.recv.at[k],
            device_id=at(*self.here, **off),
            device_id_type=MESH,
        )
        copy.start()
        self.open.append(copy)
        return copy

    def drain(self):
        for copy in self.open:
            copy.wait_send()


def turn(values, block, table):
    cr, sr = table[pl.ds(0, BLK), :], table[pl.ds(BLK, BLK), :]
    c0 = table[pl.ds(2 * BLK + block, 1), :]
    s0 = table[pl.ds(2 * BLK + 64 + block, 1), :]
    cosine = c0 * cr - s0 * sr
    sine = s0 * cr + c0 * sr
    return values * cosine + pltpu.roll(values, HEAD // 2, 1) * sine


OFFSETS = [
    dict(dx=1),
    dict(dx=3),
    dict(dx=2),
    dict(dy=1),
    dict(dy=3),
    dict(dz=1),
    dict(dz=3),
    dict(dz=2),
    dict(dc=1),
]


def layer_kernel(
    order, where, lengths, table_hbm, tok_hbm, wq, wkv_hbm, wo_hbm, out,
    table, tok, wkv, wo, tx, wy, kv, kv_mine, kv_sib_s, kv_sib_r, kv_z_s, kv_z_r,
    q_mine, q_sib_s, q_sib_r, q_z_s, q_z_r, q, score, away, att, acc, local, send, recv,
):
    here = place()
    y, x, z, c = here
    s = 4 * y + x
    loads = [
        pltpu.make_async_copy(src, dst, local.at[k])
        for k, (src, dst) in enumerate(
            ((tok_hbm, tok), (wkv_hbm, wkv), (table_hbm, table), (wq, wy.at[y]), (wo_hbm, wo))
        )
    ]
    for load in loads:
        load.start()
    greet(here, OFFSETS)
    go = Copies(here, send, recv)
    top, low = pl.ds(0, HALF), pl.ds(HALF, HALF)
    wtop, wlow = pl.ds(0, WIDTH // 2), pl.ds(WIDTH // 2, WIDTH // 2)

    t_up_t = go.start(tok_hbm.at[top], tx.at[0, top], dx=1)
    t_dn_l = go.start(tok_hbm.at[low], tx.at[1, low], dx=3)
    w_up_t = go.start(wq.at[wtop], wy.at[y, wtop], dy=1)
    w_dn_l = go.start(wq.at[wlow], wy.at[y, wlow], dy=3)
    w_up_l = go.start(wq.at[wlow], wy.at[y, wlow], dy=1)
    w_dn_t = go.start(wq.at[wtop], wy.at[y, wtop], dy=3)

    def pair_part(half, into):
        rows = tok[pl.ds(pl.multiple_of(half * HALF, HALF), HALF), :]
        for g in range(4):
            part = jnp.dot(rows, wkv[:, pl.ds(g * 256, 256)], preferred_element_type=F32)
            for i in range(2):
                h = 2 * g + i
                into[h % 4, :, pl.ds((h // 4) * HEAD, HEAD)] = part[:, i * HEAD : (i + 1) * HEAD].astype(into.dtype)

    loads[0].wait()
    loads[1].wait()
    pair_part(1 - c, kv_sib_s)
    sib = go.start(kv_sib_s, kv_sib_r, dc=1)
    pair_part(c, kv_mine)
    sib.wait_recv()
    kv_z = []
    for r in (2, 1, 3):
        d = (z + r) % 4
        kv_z_s[r - 1] = (kv_mine[d] + kv_sib_r[d].astype(F32)).astype(BF16)
        kv_z.append(go.start(kv_z_s.at[r - 1], kv_z_r.at[r - 1], dz=r))
    loads[2].wait()
    loads[3].wait()
    for copy in kv_z:
        copy.wait_recv()
    own_pair = kv_mine[z] + kv_sib_r[z].astype(F32)
    for r in range(3):
        own_pair = own_pair + kv_z_r[r].astype(F32)
    for i in range(2):
        part = own_pair[i * BLK : (i + 1) * BLK]
        kv[32 * c + 2 * s + i, :, pl.ds(0, HEAD)] = turn(part[:, :HEAD], order[4 * s + 2 * c + i], table).astype(BF16)
        kv[32 * c + 2 * s + i, :, pl.ds(HEAD, HEAD)] = part[:, HEAD:].T.astype(BF16)

    def blocks(dy, column, n):
        return kv.at[pl.ds(32 * c + 8 * ((y + dy) % 4) + 2 * column, 2 * n)]

    own = blocks(0, x, 1)
    kv_x = {r: go.start(own, own, dx=r) for r in (1, 3, 2)}

    def kv_along_y(r):
        piece = blocks(0, (x + 4 - r) % 4, 1)
        return go.start(piece, piece, dy=1), go.start(piece, piece, dy=3)

    kv_y = {0: kv_along_y(0)}
    t_up_l = go.start(tok_hbm.at[low], tx.at[0, low], dx=1)
    t_dn_t = go.start(tok_hbm.at[top], tx.at[1, top], dx=3)

    w_up_t.wait_recv()
    piece = wy.at[(y + 3) % 4, wtop]
    w_rel_up = go.start(piece, piece, dy=1)
    w_dn_l.wait_recv()
    piece = wy.at[(y + 1) % 4, wlow]
    w_rel_dn = go.start(piece, piece, dy=3)
    w_up_l.wait_recv()
    w_dn_t.wait_recv()

    def project(u, rows_ref):
        def one(g, carry):
            part = jnp.dot(rows_ref[...], wy[g], preferred_element_type=F32)
            first, second = part[:, :HEAD], part[:, HEAD:]
            q_mine[u, g] = jnp.where(c == 0, first, second)
            q_sib_s[u, g] = jnp.where(c == 0, second, first).astype(BF16)
            return carry

        lax.fori_loop(0, 4, one, 0)
        return go.start(q_sib_s.at[u], q_sib_r.at[u], dc=1)

    def spread(u, copy):
        copy.wait_recv()
        sent = []
        for r in (2, 1, 3):
            d = (z + r) % 4
            q_z_s[u, r - 1] = (q_mine[u, d] + q_sib_r[u, d].astype(F32)).astype(BF16)
            sent.append(go.start(q_z_s.at[u, r - 1], q_z_r.at[u, r - 1], dz=r))
        return sent

    scale = math.log2(math.e) / math.sqrt(HEAD)

    def spot_of(u, i):
        t, h = UNITS[u]
        return 4 * (4 * y + (x + SHIFT[t]) % 4) + 2 * h + i

    def block_at(u, i):
        return order[spot_of(u, i)]

    def finish(u, sent):
        for copy in sent:
            copy.wait_recv()
        for i in range(2):
            rows = pl.ds(i * BLK, BLK)
            total = q_mine[u, z, rows, :] + q_sib_r[u, z, rows, :].astype(F32)
            for r in range(3):
                total = total + q_z_r[u, r, rows, :].astype(F32)
            q[u, rows, :] = (turn(total, block_at(u, i), table) * scale).astype(BF16)

    def attend(units):
        for k, (u, i) in enumerate([(u, i) for u in units for i in range(2)]):
            block = block_at(u, i)
            query = q[u, pl.ds(i * BLK, BLK), :]
            pos = lax.broadcasted_iota(jnp.int32, (1, BLK), 1) + block * BLK
            begin = jnp.zeros((1, BLK), jnp.int32)
            end = jnp.int32(0)
            for d in range(16):
                end = end + lengths[d]
                begin = jnp.where(pos >= end, end, begin)
            row = lax.broadcasted_iota(jnp.int32, (BLK, BLK), 0)
            ahead = row - (begin - (block - (WINDOW_BLOCKS - 1)) * BLK)
            causal = row <= lax.broadcasted_iota(jnp.int32, (BLK, BLK), 1)
            largest = jnp.full((BLK, BLK), NEG, F32)
            held = [where[WINDOW_BLOCKS * spot_of(u, i) + j] for j in range(WINDOW_BLOCKS)]
            keys = jnp.concatenate([kv[n, :, pl.ds(0, HEAD)] for n in held], axis=0)
            score[k] = lax.dot_general(keys, query, (((1,), (1,)), ((), ())), preferred_element_type=F32)
            for j in range(WINDOW_BLOCKS):
                allowed = ahead >= -j * BLK
                if j == WINDOW_BLOCKS - 1:
                    allowed = allowed & causal
                v = jnp.where(allowed, score[k, pl.ds(j * BLK, BLK), :], NEG)
                score[k, pl.ds(j * BLK, BLK), :] = v
                largest = jnp.maximum(largest, v)
            largest = jnp.max(largest, axis=0, keepdims=True)
            total = jnp.zeros((BLK, BLK), F32)
            parts = []
            for j in range(WINDOW_BLOCKS):
                w = jnp.exp2(score[k, pl.ds(j * BLK, BLK), :] - largest)
                total = total + w
                parts.append(w.astype(BF16))
            weights = jnp.concatenate(parts, axis=0)
            values = jnp.concatenate([kv[n, :, pl.ds(HEAD, HEAD)] for n in held], axis=1)
            mixed = jnp.dot(values, weights, preferred_element_type=F32)
            mixed = (mixed / jnp.sum(total, axis=0, keepdims=True)).T.astype(BF16)
            t, h = UNITS[u]
            if t == 0:
                att[z, c, x, pl.ds(h * HALF + i * BLK, BLK), :] = mixed
            else:
                away[u - 2, pl.ds(i * BLK, BLK), :] = mixed

    home, lifts, relays = {}, {}, {}

    def source(t):
        return (x + 4 - SHIFT[t]) % 4

    def part_of(u):
        return pl.ds(UNITS[u][1] * HALF, HALF)

    def hop(u):
        home[u] = go.start(away.at[u - 2], att.at[z, c, x, part_of(u)], dx=SHIFT[UNITS[u][0]])

    def lift(u):
        if u in home:
            home[u].wait_recv()
        piece = att.at[z, c, source(UNITS[u][0]), part_of(u)]
        lifts[u] = go.start(piece, piece, dz=1), go.start(piece, piece, dz=3)

    def relay(u):
        t, h = UNITS[u]
        lifts[u][h].wait_recv()
        piece = att.at[(z + (1 if h else 3)) % 4, c, source(t), part_of(u)]
        relays[u] = go.start(piece, piece, dz=3 if h else 1)

    shared = {}

    def share(r, t):
        piece = att.at[(z + r) % 4, c, source(t)]
        shared[r, t] = go.start(piece, piece, dc=1)

    def units_of(t):
        return [u for u in range(8) if UNITS[u][0] == t]

    def settle(t):
        for u in units_of(t):
            lifts[u][1 - UNITS[u][1]].wait_recv()
        share(3, t)
        share(1, t)
        for u in units_of(t):
            relays[u].wait_recv()
        share(2, t)

    def product(pieces, cols):
        left = jnp.concatenate([att[d, k, source(t)] for d, t in pieces for k in range(2)], axis=1)
        right = jnp.concatenate(
            [wo[pl.ds(pl.multiple_of((4 * d + source(t)) * 256, 256), 256), cols] for d, t in pieces], axis=0
        )
        return jnp.dot(left, right, preferred_element_type=F32)

    def multiply(pieces, first):
        def tile(n, carry):
            cols = pl.ds(pl.multiple_of(n * 256, 256), 256)
            part = product(pieces, cols)
            acc[:, cols] = part if first else acc[:, cols] + part
            return carry

        lax.fori_loop(0, 4, tile, 0)

    def bring(r, ts):
        for t in ts:
            shared[r, t].wait_recv()

    row = lambda r: blocks(r, 0, 4)
    kv_sib, kv_rel = [], []

    w_rel_up.wait_recv()
    w_rel_dn.wait_recv()
    sib0 = project(0, tok.at[top])
    sib1 = project(1, tok.at[low])
    sent0 = spread(0, sib0)
    for r in (1, 3):
        kv_x[r].wait_recv()
        kv_y[r] = kv_along_y(r)
    sent1 = spread(1, sib1)
    t_up_t.wait_recv()
    sib2 = project(2, tx.at[0, top])
    t_dn_l.wait_recv()
    sib3 = project(3, tx.at[1, low])
    kv_x[2].wait_recv()
    kv_y[2] = kv_along_y(2)
    kv_sib.append(go.start(row(0), row(0), dc=1))
    t_rel_up = go.start(tx.at[0, top], tx.at[2, top], dx=1)
    t_rel_dn = go.start(tx.at[1, low], tx.at[2, low], dx=3)
    sent2 = spread(2, sib2)
    sent3 = spread(3, sib3)
    finish(0, sent0)
    finish(1, sent1)

    def kv_pass(r):
        up = r % 2 == 0
        kv_y[r][0 if up else 1].wait_recv()
        piece = blocks(3 if up else 1, (x + 4 - r) % 4, 1)
        kv_rel.append(go.start(piece, piece, dy=1 if up else 3))

    kv_pass(0)
    kv_pass(1)
    t_up_l.wait_recv()
    sib4 = project(4, tx.at[0, low])
    t_dn_t.wait_recv()
    sib5 = project(5, tx.at[1, top])
    finish(2, sent2)
    finish(3, sent3)
    kv_pass(3)
    kv_pass(2)
    sent4 = spread(4, sib4)
    sent5 = spread(5, sib5)
    for r in range(4):
        kv_y[r][1 if r % 2 == 0 else 0].wait_recv()
    kv_sib.append(go.start(row(3), row(3), dc=1))
    kv_sib.append(go.start(row(1), row(1), dc=1))
    for copy in kv_rel:
        copy.wait_recv()
    kv_sib.append(go.start(row(2), row(2), dc=1))
    for copy in kv_sib:
        copy.wait_recv()
    attend((0, 1))
    lift(0)
    lift(1)
    share(0, 0)
    t_rel_up.wait_recv()
    sib6 = project(6, tx.at[2, top])
    t_rel_dn.wait_recv()
    sib7 = project(7, tx.at[2, low])
    attend((2, 3))
    hop(2)
    hop(3)
    sent6 = spread(6, sib6)
    sent7 = spread(7, sib7)
    finish(4, sent4)
    finish(5, sent5)
    relay(0)
    relay(1)
    attend((4, 5))
    hop(4)
    hop(5)
    lift(2)
    lift(3)
    finish(6, sent6)
    finish(7, sent7)
    attend((6, 7))
    hop(6)
    hop(7)
    lift(4)
    lift(5)
    share(0, 1)
    share(0, 2)
    relay(2)
    relay(3)
    settle(0)
    loads[4].wait()
    bring(0, (0, 1, 2))
    multiply([(z, 0), (z, 1), (z, 2)], True)
    lift(6)
    lift(7)
    share(0, 3)
    relay(4)
    relay(5)
    settle(1)
    settle(2)
    for r in (1, 3, 2):
        bring(r, (0, 1, 2))
        d = (z + r) % 4
        multiply([(d, 0), (d, 1), (d, 2)], False)
        if r == 1:
            relay(6)
            relay(7)
    settle(3)
    for r in range(4):
        bring(r, (3,))
    last = [(d, 3) for d in range(4)]

    def close(n, carry):
        cols = pl.ds(pl.multiple_of(n * 256, 256), 256)
        out[:, cols] = (acc[:, cols] + product(last, cols)).astype(BF16)
        return carry

    lax.fori_loop(0, 4, close, 0)
    go.drain()


def layer(order, where, lengths, tok, wq, wkv, wo):
    vm = pl.BlockSpec(memory_space=pltpu.VMEM)
    sm = pl.BlockSpec(memory_space=pltpu.SMEM)
    hbm = pl.BlockSpec(memory_space=pl.ANY)
    n = 128
    return pl.pallas_call(
        layer_kernel,
        out_shape=jax.ShapeDtypeStruct((ROWS, WIDTH), BF16),
        in_specs=[sm] * 3 + [hbm] * 5,
        out_specs=vm,
        scratch_shapes=[
            pltpu.VMEM((3 * BLK, HEAD), F32),
            pltpu.VMEM((ROWS, WIDTH), BF16),
            pltpu.VMEM((WIDTH, WIDTH), BF16),
            pltpu.VMEM((4 * WIDTH, WIDTH), BF16),
            pltpu.VMEM((3, ROWS, WIDTH), BF16),
            pltpu.VMEM((4, WIDTH, 256), BF16),
            pltpu.VMEM((64, BLK, 256), BF16),
            pltpu.VMEM((4, 256, 256), F32),
            pltpu.VMEM((4, 256, 256), BF16),
            pltpu.VMEM((4, 256, 256), BF16),
            pltpu.VMEM((3, 256, 256), BF16),
            pltpu.VMEM((3, 256, 256), BF16),
            pltpu.VMEM((8, 4, HALF, HEAD), F32),
            pltpu.VMEM((8, 4, HALF, HEAD), BF16),
            pltpu.VMEM((8, 4, HALF, HEAD), BF16),
            pltpu.VMEM((8, 3, HALF, HEAD), BF16),
            pltpu.VMEM((8, 3, HALF, HEAD), BF16),
            pltpu.VMEM((8, HALF, HEAD), BF16),
            pltpu.VMEM((4, WINDOW_BLOCKS * BLK, BLK), F32),
            pltpu.VMEM((6, HALF, HEAD), BF16),
            pltpu.VMEM((4, 2, 4, ROWS, HEAD), BF16),
            pltpu.VMEM((ROWS, WIDTH), F32),
            pltpu.SemaphoreType.DMA((5,)),
            pltpu.SemaphoreType.DMA((n,)),
            pltpu.SemaphoreType.DMA((n,)),
        ],
        compiler_params=pltpu.CompilerParams(
            collective_id=0, has_side_effects=True, vmem_limit_bytes=60 << 20
        ),
    )(order, where, lengths, jnp.asarray(rope_tables()), tok, wq, wkv, wo)


def body(tokens, query_weight, key_value_matrix, output_weight, document_lengths, block_order):
    held = np.arange(64, dtype=np.int32)
    slot = held % 4 // 2 * 32 + held // 4 * 2 + held % 2
    wanted = jnp.maximum(block_order[:, None] + np.arange(1 - WINDOW_BLOCKS, 1, dtype=np.int32), 0)
    match = block_order[:, None] == wanted.reshape(1, -1)
    where = jnp.sum(jnp.where(match, slot[:, None], 0), axis=0)
    return layer(
        block_order, where, document_lengths, tokens, query_weight, key_value_matrix, output_weight
    )


def solution(mesh):
    placed = (P("seq", "mp"), P("mp", "seq"), P("mp", None), P(None, "mp"), P(), P())
    return jax.shard_map(
        body, mesh=mesh, in_specs=placed, out_specs=P("seq", "mp"), check_vma=False
    )
```

time: 143 us -> 98.3 us (0.69)
  Pallas kernels: 131 us -> 93.6 us
  local copies, waits for them, and re-layouts: 11.5 us -> 2.4 us
    pallas_call x3 -> x1, Pallas kernels: 131 us -> 93.6 us  [layer(): pl.pallas_call(layer_kernel, out_shape=jax.ShapeDtypeStruct((ROWS, WIDTH)...]
    unnamed x23 -> x1, local copies, waits for them, and re-layouts: 11.5 us -> 2.26 us
where the time goes in v2:
time: 98.3 us; the launch traced here: 98.1 us
  Pallas kernels  93.6 us (95%)
  local copies, waits for them, and re-layouts  2.4 us (2%)
  other arithmetic  2.13 us (2%)
    pallas_call x1, Pallas kernels, layer(): pl.pallas_call(layer_kernel, out_shape=jax.ShapeDtypeStruct((ROWS, WIDTH)...  93.6 us
    unnamed x1, local copies, waits for them, and re-layouts  2.26 us

profile of v2, /device:TPU:1, one launch (start us, length us, event | category | flops | bytes accessed | tf_op | source)
XLA Modules:
  0.0 98.1 jit_solution(474734291245961050)
XLA Ops:
  0.0 0.7 add_maximum_fusion
  0.7 0.1 max.15
  0.9 1.4 %select_reduce_fusion.where = s32[1088]{0:T(1024)} fusion(s32[64]{0:T(128)} %constant.12, s32[1088]{0:T(1024)S(1)} %max.15, s32[64]{0:T(128)} %order.1), kind=kLoop, calls=%fused_computation | loop fusion | flops 207808 | bytes 9216 | tf_op jit(solution)/shard_map/reduce_sum | solution.py:501
  2.3 93.6 %shard_map.91 = bf16[512,1024]{1,0:T(8,128)(2,1)} custom-call(s32[64]{0:T(128)} %order.1, s32[1088]{0:T(1024)} %select_reduce_fusion.where, s32[16]{0:T(128)} %lengths.1, f32[384,128]{1,0:T(8,128)} %constant.11.clone.table_hbm, bf16[512,1024]{1,0:T(8,128)(2,1)} %tok_hbm.1, bf16[1024,256]{1,0:T(8,128)(2,1)} %wq.1, bf16[1024,1024]{1,0:T(8,128)(2,1)} %wkv_hbm.1, ...), custom_call_target="tpu_custom_call" | custom-call | tf_op jit(solution)/shard_map/pallas_call | solution.py:458
  95.9 2.3 %copy.11 = bf16[512,1024]{1,0:T(8,128)(2,1)} copy(bf16[512,1024]{1,0:T(8,128)(2,1)} %shard_map.91) | data formatting | bytes 2097152

commit v3 on v2

--- a/solution.py
+++ b/solution.py
@@ -110,9 +110,9 @@
 
 
 def layer_kernel(
-    order, where, lengths, table_hbm, tok_hbm, wq, wkv_hbm, wo_hbm, out,
+    order, lengths, table_hbm, tok_hbm, wq, wkv_hbm, wo_hbm, out,
     table, tok, wkv, wo, tx, wy, kv, kv_mine, kv_sib_s, kv_sib_r, kv_z_s, kv_z_r,
-    q_mine, q_sib_s, q_sib_r, q_z_s, q_z_r, q, score, away, att, acc, local, send, recv,
+    q_mine, q_sib_s, q_sib_r, q_z_s, q_z_r, q, score, away, att, acc, windows, where, local, send, recv,
 ):
     here = place()
     y, x, z, c = here
@@ -123,7 +123,7 @@
             ((tok_hbm, tok), (wkv_hbm, wkv), (table_hbm, table), (wq, wy.at[y]), (wo_hbm, wo))
         )
     ]
-    for load in loads:
+    for load in loads[:4]:
         load.start()
     greet(here, OFFSETS)
     go = Copies(here, send, recv)
@@ -156,8 +156,32 @@
         d = (z + r) % 4
         kv_z_s[r - 1] = (kv_mine[d] + kv_sib_r[d].astype(F32)).astype(BF16)
         kv_z.append(go.start(kv_z_s.at[r - 1], kv_z_r.at[r - 1], dz=r))
+    loads[4].start()
+    lane = lax.broadcasted_iota(jnp.int32, (16, BLK), 1)
+    line = lax.broadcasted_iota(jnp.int32, (16, BLK), 0)
+    wanted = lane - (WINDOW_BLOCKS - 1)
+    for n in range(16):
+        t, h = UNITS[n // 2]
+        mine = order[4 * (4 * y + (x + SHIFT[t]) % 4) + 2 * h + n % 2]
+        wanted = wanted + jnp.where(line == n, mine, 0)
+    wanted = jnp.maximum(wanted, 0)
+    found = jnp.zeros((16, BLK), jnp.int32)
+    for n in range(64):
+        found = jnp.where(wanted == order[n], n % 4 // 2 * 32 + n // 4 * 2 + n % 2, found)
+    windows[...] = found
+    table_copy = pltpu.make_async_copy(windows, where, local.at[5])
+    table_copy.start()
     loads[2].wait()
     loads[3].wait()
+    table_copy.wait()
+    w_up_t.wait_recv()
+    piece = wy.at[(y + 3) % 4, wtop]
+    w_rel_up = go.start(piece, piece, dy=1)
+    w_dn_l.wait_recv()
+    piece = wy.at[(y + 1) % 4, wlow]
+    w_rel_dn = go.start(piece, piece, dy=3)
+    w_up_l.wait_recv()
+    w_dn_t.wait_recv()
     for copy in kv_z:
         copy.wait_recv()
     own_pair = kv_mine[z] + kv_sib_r[z].astype(F32)
@@ -179,17 +203,6 @@
         return go.start(piece, piece, dy=1), go.start(piece, piece, dy=3)
 
     kv_y = {0: kv_along_y(0)}
-    t_up_l = go.start(tok_hbm.at[low], tx.at[0, low], dx=1)
-    t_dn_t = go.start(tok_hbm.at[top], tx.at[1, top], dx=3)
-
-    w_up_t.wait_recv()
-    piece = wy.at[(y + 3) % 4, wtop]
-    w_rel_up = go.start(piece, piece, dy=1)
-    w_dn_l.wait_recv()
-    piece = wy.at[(y + 1) % 4, wlow]
-    w_rel_dn = go.start(piece, piece, dy=3)
-    w_up_l.wait_recv()
-    w_dn_t.wait_recv()
 
     def project(u, rows_ref):
         def one(g, carry):
@@ -244,7 +257,7 @@
             ahead = row - (begin - (block - (WINDOW_BLOCKS - 1)) * BLK)
             causal = row <= lax.broadcasted_iota(jnp.int32, (BLK, BLK), 1)
             largest = jnp.full((BLK, BLK), NEG, F32)
-            held = [where[WINDOW_BLOCKS * spot_of(u, i) + j] for j in range(WINDOW_BLOCKS)]
+            held = [where[2 * u + i, j] for j in range(WINDOW_BLOCKS)]
             keys = jnp.concatenate([kv[n, :, pl.ds(0, HEAD)] for n in held], axis=0)
             score[k] = lax.dot_general(keys, query, (((1,), (1,)), ((), ())), preferred_element_type=F32)
             for j in range(WINDOW_BLOCKS):
@@ -326,7 +339,7 @@
             acc[:, cols] = part if first else acc[:, cols] + part
             return carry
 
-        lax.fori_loop(0, 4, tile, 0)
+        lax.fori_loop(0, 4, tile, 0, unroll=2)
 
     def bring(r, ts):
         for t in ts:
@@ -334,29 +347,6 @@
 
     row = lambda r: blocks(r, 0, 4)
     kv_sib, kv_rel = [], []
-
-    w_rel_up.wait_recv()
-    w_rel_dn.wait_recv()
-    sib0 = project(0, tok.at[top])
-    sib1 = project(1, tok.at[low])
-    sent0 = spread(0, sib0)
-    for r in (1, 3):
-        kv_x[r].wait_recv()
-        kv_y[r] = kv_along_y(r)
-    sent1 = spread(1, sib1)
-    t_up_t.wait_recv()
-    sib2 = project(2, tx.at[0, top])
-    t_dn_l.wait_recv()
-    sib3 = project(3, tx.at[1, low])
-    kv_x[2].wait_recv()
-    kv_y[2] = kv_along_y(2)
-    kv_sib.append(go.start(row(0), row(0), dc=1))
-    t_rel_up = go.start(tx.at[0, top], tx.at[2, top], dx=1)
-    t_rel_dn = go.start(tx.at[1, low], tx.at[2, low], dx=3)
-    sent2 = spread(2, sib2)
-    sent3 = spread(3, sib3)
-    finish(0, sent0)
-    finish(1, sent1)
 
     def kv_pass(r):
         up = r % 2 == 0
@@ -364,22 +354,40 @@
         piece = blocks(3 if up else 1, (x + 4 - r) % 4, 1)
         kv_rel.append(go.start(piece, piece, dy=1 if up else 3))
 
+    w_rel_up.wait_recv()
+    w_rel_dn.wait_recv()
+    sib0 = project(0, tok.at[top])
+    for r in (1, 3):
+        kv_x[r].wait_recv()
+        kv_y[r] = kv_along_y(r)
+    t_up_l = go.start(tok_hbm.at[low], tx.at[0, low], dx=1)
+    t_dn_t = go.start(tok_hbm.at[top], tx.at[1, top], dx=3)
+    kv_x[2].wait_recv()
+    kv_y[2] = kv_along_y(2)
+    kv_sib.append(go.start(row(0), row(0), dc=1))
+    sib1 = project(1, tok.at[low])
+    spread0 = spread(0, sib0)
     kv_pass(0)
     kv_pass(1)
-    t_up_l.wait_recv()
-    sib4 = project(4, tx.at[0, low])
-    t_dn_t.wait_recv()
-    sib5 = project(5, tx.at[1, top])
-    finish(2, sent2)
-    finish(3, sent3)
+    t_up_t.wait_recv()
+    sib2 = project(2, tx.at[0, top])
+    spread1 = spread(1, sib1)
+    t_dn_l.wait_recv()
+    t_rel_up = go.start(tx.at[0, top], tx.at[2, top], dx=1)
+    t_rel_dn = go.start(tx.at[1, low], tx.at[2, low], dx=3)
+    sib3 = project(3, tx.at[1, low])
+    spread2 = spread(2, sib2)
     kv_pass(3)
+    spread3 = spread(3, sib3)
     kv_pass(2)
-    sent4 = spread(4, sib4)
-    sent5 = spread(5, sib5)
+    finish(0, spread0)
+    finish(1, spread1)
     for r in range(4):
         kv_y[r][1 if r % 2 == 0 else 0].wait_recv()
     kv_sib.append(go.start(row(3), row(3), dc=1))
     kv_sib.append(go.start(row(1), row(1), dc=1))
+    finish(2, spread2)
+    finish(3, spread3)
     for copy in kv_rel:
         copy.wait_recv()
     kv_sib.append(go.start(row(2), row(2), dc=1))
@@ -389,53 +397,61 @@
     lift(0)
     lift(1)
     share(0, 0)
-    t_rel_up.wait_recv()
-    sib6 = project(6, tx.at[2, top])
-    t_rel_dn.wait_recv()
-    sib7 = project(7, tx.at[2, low])
+    t_up_l.wait_recv()
+    sib4 = project(4, tx.at[0, low])
+    t_dn_t.wait_recv()
+    sib5 = project(5, tx.at[1, top])
     attend((2, 3))
     hop(2)
     hop(3)
-    sent6 = spread(6, sib6)
-    sent7 = spread(7, sib7)
-    finish(4, sent4)
-    finish(5, sent5)
+    spread4 = spread(4, sib4)
+    spread5 = spread(5, sib5)
     relay(0)
     relay(1)
+    t_rel_up.wait_recv()
+    sib6 = project(6, tx.at[2, top])
+    lift(2)
+    lift(3)
+    t_rel_dn.wait_recv()
+    sib7 = project(7, tx.at[2, low])
+    spread6 = spread(6, sib6)
+    finish(4, spread4)
+    finish(5, spread5)
+    spread7 = spread(7, sib7)
     attend((4, 5))
     hop(4)
     hop(5)
-    lift(2)
-    lift(3)
-    finish(6, sent6)
-    finish(7, sent7)
-    attend((6, 7))
-    hop(6)
-    hop(7)
+    relay(2)
+    relay(3)
+    settle(0)
     lift(4)
     lift(5)
     share(0, 1)
     share(0, 2)
-    relay(2)
-    relay(3)
-    settle(0)
     loads[4].wait()
-    bring(0, (0, 1, 2))
-    multiply([(z, 0), (z, 1), (z, 2)], True)
+    for r in range(4):
+        bring(r, (0,))
+    multiply([(d, 0) for d in range(4)], True)
+    finish(6, spread6)
+    finish(7, spread7)
+    attend((6, 7))
+    hop(6)
+    hop(7)
+    relay(4)
+    relay(5)
     lift(6)
     lift(7)
     share(0, 3)
-    relay(4)
-    relay(5)
     settle(1)
+    for r in range(4):
+        bring(r, (1,))
+    multiply([(d, 1) for d in range(4)], False)
     settle(2)
-    for r in (1, 3, 2):
-        bring(r, (0, 1, 2))
-        d = (z + r) % 4
-        multiply([(d, 0), (d, 1), (d, 2)], False)
-        if r == 1:
-            relay(6)
-            relay(7)
+    for r in range(4):
+        bring(r, (2,))
+    relay(6)
+    relay(7)
+    multiply([(d, 2) for d in range(4)], False)
     settle(3)
     for r in range(4):
         bring(r, (3,))
@@ -450,7 +466,7 @@
     go.drain()
 
 
-def layer(order, where, lengths, tok, wq, wkv, wo):
+def layer(order, lengths, tok, wq, wkv, wo):
     vm = pl.BlockSpec(memory_space=pltpu.VMEM)
     sm = pl.BlockSpec(memory_space=pltpu.SMEM)
     hbm = pl.BlockSpec(memory_space=pl.ANY)
@@ -458,7 +474,7 @@
     return pl.pallas_call(
         layer_kernel,
         out_shape=jax.ShapeDtypeStruct((ROWS, WIDTH), BF16),
-        in_specs=[sm] * 3 + [hbm] * 5,
+        in_specs=[sm] * 2 + [hbm] * 5,
         out_specs=vm,
         scratch_shapes=[
             pltpu.VMEM((3 * BLK, HEAD), F32),
@@ -483,24 +499,21 @@
             pltpu.VMEM((6, HALF, HEAD), BF16),
             pltpu.VMEM((4, 2, 4, ROWS, HEAD), BF16),
             pltpu.VMEM((ROWS, WIDTH), F32),
-            pltpu.SemaphoreType.DMA((5,)),
+            pltpu.VMEM((16, BLK), jnp.int32),
+            pltpu.SMEM((16, BLK), jnp.int32),
+            pltpu.SemaphoreType.DMA((6,)),
             pltpu.SemaphoreType.DMA((n,)),
             pltpu.SemaphoreType.DMA((n,)),
         ],
         compiler_params=pltpu.CompilerParams(
-            collective_id=0, has_side_effects=True, vmem_limit_bytes=60 << 20
+            collective_id=0, has_side_effects=True, vmem_limit_bytes=54 << 20
         ),
-    )(order, where, lengths, jnp.asarray(rope_tables()), tok, wq, wkv, wo)
+    )(order, lengths, jnp.asarray(rope_tables()), tok, wq, wkv, wo)
 
 
 def body(tokens, query_weight, key_value_matrix, output_weight, document_lengths, block_order):
-    held = np.arange(64, dtype=np.int32)
-    slot = held % 4 // 2 * 32 + held // 4 * 2 + held % 2
-    wanted = jnp.maximum(block_order[:, None] + np.arange(1 - WINDOW_BLOCKS, 1, dtype=np.int32), 0)
-    match = block_order[:, None] == wanted.reshape(1, -1)
-    where = jnp.sum(jnp.where(match, slot[:, None], 0), axis=0)
     return layer(
-        block_order, where, document_lengths, tokens, query_weight, key_value_matrix, output_weight
+        block_order, document_lengths, tokens, query_weight, key_value_matrix, output_weight
     )
 
 

time: 98.3 us -> 97 us (0.987)
  other arithmetic: 2.13 us -> 0 us
  Pallas kernels: 93.6 us -> 94.6 us
    reduce_sum x1 -> x0, other arithmetic: 1.38 us -> none  [body(): where = jnp.sum(jnp.where(match, slot[:, None], 0), axis=0)]
    pallas_call x1, Pallas kernels: 93.6 us -> 94.6 us  [layer(): pl.pallas_call(layer_kernel, out_shape=jax.ShapeDtypeStruct((ROWS, WIDTH)...]
where the time goes in v3:
time: 97 us; the launch traced here: 96.9 us
  Pallas kernels  94.6 us (98%)
  local copies, waits for them, and re-layouts  2.26 us (2%)
    pallas_call x1, Pallas kernels, layer(): pl.pallas_call(layer_kernel, out_shape=jax.ShapeDtypeStruct((ROWS, WIDTH)...  94.6 us
    unnamed x1, local copies, waits for them, and re-layouts  2.26 us

profile of v3, /device:TPU:1, one launch (start us, length us, event | category | flops | bytes accessed | tf_op | source)
XLA Modules:
  0.0 96.9 jit_solution(13453517696467255685)
XLA Ops:
  0.0 94.6 %shard_map.73 = bf16[512,1024]{1,0:T(8,128)(2,1)} custom-call(s32[64]{0:T(128)} %order.1, s32[16]{0:T(128)} %lengths.1, f32[384,128]{1,0:T(8,128)} %constant.2.clone.table_hbm, bf16[512,1024]{1,0:T(8,128)(2,1)} %tok_hbm.1, bf16[1024,256]{1,0:T(8,128)(2,1)} %wq.1, bf16[1024,1024]{1,0:T(8,128)(2,1)} %wkv_hbm.1, bf16[4096,1024]{1,0:T(8,128)(2,1)} %wo_hbm.1), custom_call_target="tpu_custom_call" | custom-call | tf_op jit(solution)/shard_map/pallas_call | solution.py:474
  94.6 2.3 %copy.9 = bf16[512,1024]{1,0:T(8,128)(2,1)} copy(bf16[512,1024]{1,0:T(8,128)(2,1)} %shard_map.73) | data formatting | bytes 2097152

commit v4 on v3

--- a/solution.py
+++ b/solution.py
@@ -212,7 +212,7 @@
             q_sib_s[u, g] = jnp.where(c == 0, second, first).astype(BF16)
             return carry
 
-        lax.fori_loop(0, 4, one, 0)
+        lax.fori_loop(0, 4, one, 0, unroll=2)
         return go.start(q_sib_s.at[u], q_sib_r.at[u], dc=1)
 
     def spread(u, copy):
@@ -299,6 +299,8 @@
         if u in home:
             home[u].wait_recv()
         piece = att.at[z, c, source(UNITS[u][0]), part_of(u)]
+        if u >= 6:
+            relays[u] = go.start(piece, piece, dz=2)
         lifts[u] = go.start(piece, piece, dz=1), go.start(piece, piece, dz=3)
 
     def relay(u):
@@ -319,6 +321,8 @@
     def settle(t):
         for u in units_of(t):
             lifts[u][1 - UNITS[u][1]].wait_recv()
+            if u >= 6:
+                lifts[u][UNITS[u][1]].wait_recv()
         share(3, t)
         share(1, t)
         for u in units_of(t):
@@ -386,62 +390,62 @@
         kv_y[r][1 if r % 2 == 0 else 0].wait_recv()
     kv_sib.append(go.start(row(3), row(3), dc=1))
     kv_sib.append(go.start(row(1), row(1), dc=1))
+    t_up_l.wait_recv()
+    sib4 = project(4, tx.at[0, low])
+    t_dn_t.wait_recv()
+    sib5 = project(5, tx.at[1, top])
     finish(2, spread2)
     finish(3, spread3)
     for copy in kv_rel:
         copy.wait_recv()
     kv_sib.append(go.start(row(2), row(2), dc=1))
+    spread4 = spread(4, sib4)
+    spread5 = spread(5, sib5)
     for copy in kv_sib:
         copy.wait_recv()
     attend((0, 1))
     lift(0)
     lift(1)
     share(0, 0)
-    t_up_l.wait_recv()
-    sib4 = project(4, tx.at[0, low])
-    t_dn_t.wait_recv()
-    sib5 = project(5, tx.at[1, top])
+    t_rel_up.wait_recv()
+    sib6 = project(6, tx.at[2, top])
+    t_rel_dn.wait_recv()
+    sib7 = project(7, tx.at[2, low])
+    spread6 = spread(6, sib6)
+    spread7 = spread(7, sib7)
     attend((2, 3))
     hop(2)
     hop(3)
-    spread4 = spread(4, sib4)
-    spread5 = spread(5, sib5)
     relay(0)
     relay(1)
-    t_rel_up.wait_recv()
-    sib6 = project(6, tx.at[2, top])
-    lift(2)
-    lift(3)
-    t_rel_dn.wait_recv()
-    sib7 = project(7, tx.at[2, low])
-    spread6 = spread(6, sib6)
     finish(4, spread4)
     finish(5, spread5)
-    spread7 = spread(7, sib7)
     attend((4, 5))
     hop(4)
     hop(5)
-    relay(2)
-    relay(3)
-    settle(0)
-    lift(4)
-    lift(5)
-    share(0, 1)
-    share(0, 2)
-    loads[4].wait()
-    for r in range(4):
-        bring(r, (0,))
-    multiply([(d, 0) for d in range(4)], True)
+    lift(2)
+    lift(3)
     finish(6, spread6)
     finish(7, spread7)
     attend((6, 7))
     hop(6)
     hop(7)
-    relay(4)
-    relay(5)
+    lift(4)
+    lift(5)
+    share(0, 1)
+    share(0, 2)
+    relay(2)
+    relay(3)
     lift(6)
     lift(7)
     share(0, 3)
+    settle(0)
+    loads[4].wait()
+    for r in range(4):
+        bring(r, (0,))
+    multiply([(d, 0) for d in range(4)], True)
+    relay(4)
+    relay(5)
     settle(1)
     for r in range(4):
         bring(r, (1,))
@@ -449,8 +453,6 @@
     settle(2)
     for r in range(4):
         bring(r, (2,))
-    relay(6)
-    relay(7)
     multiply([(d, 2) for d in range(4)], False)
     settle(3)
     for r in range(4):
@@ -462,7 +464,7 @@
         out[:, cols] = (acc[:, cols] + product(last, cols)).astype(BF16)
         return carry
 
-    lax.fori_loop(0, 4, close, 0)
+    lax.fori_loop(0, 4, close, 0, unroll=2)
     go.drain()
 
 
@@ -470,7 +472,7 @@
     vm = pl.BlockSpec(memory_space=pltpu.VMEM)
     sm = pl.BlockSpec(memory_space=pltpu.SMEM)
     hbm = pl.BlockSpec(memory_space=pl.ANY)
-    n = 128
+    n = 136
     return pl.pallas_call(
         layer_kernel,
         out_shape=jax.ShapeDtypeStruct((ROWS, WIDTH), BF16),

time: 97 us -> 93 us (0.959)
  Pallas kernels: 94.6 us -> 90.6 us
    pallas_call x1, Pallas kernels: 94.6 us -> 90.6 us  [layer(): pl.pallas_call(layer_kernel, out_shape=jax.ShapeDtypeStruct((ROWS, WIDTH)...]
where the time goes in v4:
time: 93 us; the launch traced here: 92.9 us
  Pallas kernels  90.6 us (97%)
  local copies, waits for them, and re-layouts  2.26 us (2%)
    pallas_call x1, Pallas kernels, layer(): pl.pallas_call(layer_kernel, out_shape=jax.ShapeDtypeStruct((ROWS, WIDTH)...  90.6 us
    unnamed x1, local copies, waits for them, and re-layouts  2.26 us

profile of v4, /device:TPU:1, one launch (start us, length us, event | category | flops | bytes accessed | tf_op | source)
XLA Modules:
  0.0 92.9 jit_solution(5209600616351144230)
XLA Ops:
  0.0 90.6 %shard_map.73 = bf16[512,1024]{1,0:T(8,128)(2,1)} custom-call(s32[64]{0:T(128)} %order.1, s32[16]{0:T(128)} %lengths.1, f32[384,128]{1,0:T(8,128)} %constant.2.clone.table_hbm, bf16[512,1024]{1,0:T(8,128)(2,1)} %tok_hbm.1, bf16[1024,256]{1,0:T(8,128)(2,1)} %wq.1, bf16[1024,1024]{1,0:T(8,128)(2,1)} %wkv_hbm.1, bf16[4096,1024]{1,0:T(8,128)(2,1)} %wo_hbm.1), custom_call_target="tpu_custom_call" | custom-call | tf_op jit(solution)/shard_map/pallas_call | solution.py:476
  90.6 2.3 %copy.9 = bf16[512,1024]{1,0:T(8,128)(2,1)} copy(bf16[512,1024]{1,0:T(8,128)(2,1)} %shard_map.73) | data formatting | bytes 2097152

commit v5 on v4

--- a/solution.py
+++ b/solution.py
@@ -212,7 +212,7 @@
             q_sib_s[u, g] = jnp.where(c == 0, second, first).astype(BF16)
             return carry
 
-        lax.fori_loop(0, 4, one, 0, unroll=2)
+        lax.fori_loop(0, 4, one, 0, unroll=4)
         return go.start(q_sib_s.at[u], q_sib_r.at[u], dc=1)
 
     def spread(u, copy):
@@ -343,7 +343,7 @@
             acc[:, cols] = part if first else acc[:, cols] + part
             return carry
 
-        lax.fori_loop(0, 4, tile, 0, unroll=2)
+        lax.fori_loop(0, 4, tile, 0, unroll=4)
 
     def bring(r, ts):
         for t in ts:
@@ -464,7 +464,7 @@
         out[:, cols] = (acc[:, cols] + product(last, cols)).astype(BF16)
         return carry
 
-    lax.fori_loop(0, 4, close, 0, unroll=2)
+    lax.fori_loop(0, 4, close, 0, unroll=4)
     go.drain()
 
 

time: 93 us -> 91.6 us (0.985)
  Pallas kernels: 90.6 us -> 89.2 us
    pallas_call x1, Pallas kernels: 90.6 us -> 89.2 us  [layer(): pl.pallas_call(layer_kernel, out_shape=jax.ShapeDtypeStruct((ROWS, WIDTH)...]
where the time goes in v5:
time: 91.6 us; the launch traced here: 91.4 us
  Pallas kernels  89.2 us (97%)
  local copies, waits for them, and re-layouts  2.26 us (2%)
    pallas_call x1, Pallas kernels, layer(): pl.pallas_call(layer_kernel, out_shape=jax.ShapeDtypeStruct((ROWS, WIDTH)...  89.2 us
    unnamed x1, local copies, waits for them, and re-layouts  2.26 us

profile of v5, /device:TPU:1, one launch (start us, length us, event | category | flops | bytes accessed | tf_op | source)
XLA Modules:
  0.0 91.4 jit_solution(5001653884742340093)
XLA Ops:
  0.0 89.2 %shard_map.73 = bf16[512,1024]{1,0:T(8,128)(2,1)} custom-call(s32[64]{0:T(128)} %order.1, s32[16]{0:T(128)} %lengths.1, f32[384,128]{1,0:T(8,128)} %constant.2.clone.table_hbm, bf16[512,1024]{1,0:T(8,128)(2,1)} %tok_hbm.1, bf16[1024,256]{1,0:T(8,128)(2,1)} %wq.1, bf16[1024,1024]{1,0:T(8,128)(2,1)} %wkv_hbm.1, bf16[4096,1024]{1,0:T(8,128)(2,1)} %wo_hbm.1), custom_call_target="tpu_custom_call" | custom-call | tf_op jit(solution)/shard_map/pallas_call | solution.py:476
  89.2 2.3 %copy.9 = bf16[512,1024]{1,0:T(8,128)(2,1)} copy(bf16[512,1024]{1,0:T(8,128)(2,1)} %shard_map.73) | data formatting | bytes 2097152
